TPU v7x, 32 devices: a whole 2x2x4 slice. The times are simulated.
32 devices in a mesh: row: 8 (over y, x, core), col: 4 (over z).
Axes of the slice: x: 2, y: 2, z: 4, core: 2. Of those that a mesh axis runs over, the one named last changes fastest.
Arguments:
- samples: bfloat16 [8192, 768], P(('row', 'col')), may hold values from -8 to 8, as said below
Outputs:
- factored: float32 [8192, 8192], P('row', 'col')
Inputs may be any that keep to these rules, and one draw needn't show every extreme that they name: `samples`: every entry is a feature value.
All inputs are finite; a program needn't handle non-finite values.
Results may differ from a plain program's by a relative error of at most 0.0003.
Values may be sent and summed in bfloat16 or wider, within the bound.
A program may use at most 128 MiB of HBM per device.

v0:
```python
import functools
import math

import jax
import jax.numpy as jnp
from jax import lax
from jax.experimental import pallas as pl
from jax.experimental.pallas import tpu as pltpu
from jax.sharding import PartitionSpec as P

PANEL = 512
LAYERS = 8
CHUNK_ROWS = 64
CHUNK_COLS = 128
TILE_ROWS = 256
TILE_COLS = 512
FACTOR = 128
STRIP = 32
INV_PI = 1.0 / math.pi
ACOS = (
    1.5707963050,
    -0.2145988016,
    0.0889789874,
    -0.0501743046,
    0.0308918810,
    -0.0170881256,
    0.0066700901,
    -0.0012624911,
)
ACOS_PI = tuple(c * INV_PI for c in ACOS)
VMEM_LIMIT = 48 * 1024 * 1024
HIGHEST = lax.Precision.HIGHEST
NT = (((1,), (1,)), ((), ()))
TN = (((0,), (0,)), ((), ()))


def angle_parts(size):
    gap = jnp.maximum(1.0 - size, 1e-30)
    root = gap * lax.rsqrt(gap)
    poly = jnp.full_like(size, ACOS_PI[-1])
    for coefficient in ACOS_PI[-2::-1]:
        poly = poly * size + coefficient
    wide = size * (INV_PI * INV_PI) + (INV_PI * INV_PI)
    sine = root * (wide * lax.rsqrt(wide))
    return root * poly, sine


def tangent_of(raw, on_diag):
    cosine = jnp.where(on_diag, 1.0, raw)
    tangent = raw
    turn, sine = angle_parts(jnp.abs(cosine))
    keep = jnp.where(cosine < 0.0, turn, 1.0 - turn)
    cosine = sine + keep * cosine
    tangent = cosine + tangent * keep
    for _ in range(LAYERS - 1):
        turn, sine = angle_parts(cosine)
        keep = 1.0 - turn
        cosine = sine + keep * cosine
        tangent = cosine + tangent * keep
    return tangent


def ntk_chunk(gram, inv_row, inv_col, len_row, len_col, row_ids, col_ids):
    on_diag = row_ids == col_ids
    raw = gram * inv_row * inv_col
    value = tangent_of(raw, on_diag) * (len_row * len_col)
    return value + jnp.where(on_diag, 1.0, 0.0)


def lengths(feats):
    wide = feats.astype(jnp.float32)
    total = jnp.sum(wide * wide, axis=1)
    scale = math.sqrt(feats.shape[1] * (LAYERS + 1.0))
    return lax.rsqrt(total), jnp.sqrt(total) * (1.0 / scale)


def factor_strip(strip, first):
    place = lax.broadcasted_iota(jnp.int32, (STRIP, 1), 0)
    for j in range(STRIP):
        lane = first + j
        inv = lax.rsqrt(strip[j : j + 1, lane : lane + 1])
        unit = strip[j : j + 1, :] * inv
        col = strip[:, lane : lane + 1] * inv
        col = jnp.where(place > j, col, jnp.where(place == j, col - 1.0, 0.0))
        strip = strip - col * unit
    return strip


def panel_kernel(
    feats, inv_row, inv_col, len_row, len_col, row_ids, col_ids, after, out, work, both
):
    rows = feats.shape[0]
    work[...] = lax.dot_general(
        feats[...], feats[:PANEL, :], NT, preferred_element_type=jnp.float32
    )
    across = PANEL // CHUNK_COLS

    def chunk(k, carry):
        r = k // across
        c = k % across
        needed = jnp.logical_or(
            r * CHUNK_ROWS >= PANEL, (r * CHUNK_ROWS) // FACTOR <= (c * CHUNK_COLS) // FACTOR
        )

        @pl.when(needed)
        def _():
            rs = pl.ds(pl.multiple_of(r * CHUNK_ROWS, CHUNK_ROWS), CHUNK_ROWS)
            cs = pl.ds(pl.multiple_of(c * CHUNK_COLS, CHUNK_COLS), CHUNK_COLS)
            work[rs, cs] = ntk_chunk(
                work[rs, cs], inv_row[rs, :], inv_col[:, cs], len_row[rs, :], len_col[:, cs],
                row_ids[rs, :], col_ids[:, cs],
            )

        return carry

    lax.fori_loop(0, rows // CHUNK_ROWS * across, chunk, 0)
    eye = jnp.where(
        lax.broadcasted_iota(jnp.int32, (FACTOR, FACTOR), 0)
        == lax.broadcasted_iota(jnp.int32, (FACTOR, FACTOR), 1),
        1.0,
        0.0,
    )
    for start in range(0, PANEL, FACTOR):
        stop = start + FACTOR
        both[:, :FACTOR] = work[start:stop, start:stop]
        both[:, FACTOR:] = eye
        for first in range(0, FACTOR, STRIP):
            strip = factor_strip(both[first : first + STRIP, :], first)
            both[first : first + STRIP, :] = strip
            last = first + STRIP
            if last < FACTOR:
                change = lax.dot_general(
                    strip[:, :FACTOR], strip, TN, precision=HIGHEST,
                    preferred_element_type=jnp.float32,
                )
                both[last:, :] = both[last:, :] - change[last:, :]
        inverse = both[:, FACTOR:]
        solved = lax.dot_general(
            work[PANEL:, start:stop], inverse, NT, precision=HIGHEST,
            preferred_element_type=jnp.float32,
        )
        out[:, start:stop] = solved
        if stop < PANEL:
            upper = jnp.dot(
                inverse, work[start:stop, stop:], precision=HIGHEST,
                preferred_element_type=jnp.float32,
            )
            work[stop:PANEL, stop:] = work[stop:PANEL, stop:] - lax.dot_general(
                upper, upper, TN, precision=HIGHEST, preferred_element_type=jnp.float32
            )
            work[PANEL:, stop:] = work[PANEL:, stop:] - jnp.dot(
                solved, upper, precision=HIGHEST, preferred_element_type=jnp.float32
            )


def in_order(pieces):
    shares, blocks = pieces.shape[:2]
    return jnp.concatenate([pieces[s, b] for b in range(blocks) for s in range(shares)], axis=0)


def ntk_kernel(
    row_block, col_block, row_feats, col_feats, inv_row, inv_col, len_row, len_col,
    row_ids, col_ids, after, out,
):
    tile_rows, tile_cols = out.shape
    top = pl.program_id(0) * tile_rows
    left = pl.program_id(1) * tile_cols
    across = tile_cols // CHUNK_COLS

    @pl.when((top + tile_rows - 1) // row_block >= left // col_block)
    def _():
        out[...] = lax.dot_general(
            row_feats[...], in_order(col_feats), NT, preferred_element_type=jnp.float32
        )

        def chunk(k, carry):
            r = (k // across) * CHUNK_ROWS
            c = (k % across) * CHUNK_COLS
            below = (top + r + CHUNK_ROWS - 1) // row_block >= (left + c) // col_block
            beyond = left + c + CHUNK_COLS > col_block

            @pl.when(jnp.logical_and(below, beyond))
            def _():
                rs = pl.ds(pl.multiple_of(r, CHUNK_ROWS), CHUNK_ROWS)
                cs = pl.ds(pl.multiple_of(c, CHUNK_COLS), CHUNK_COLS)
                out[rs, cs] = ntk_chunk(
                    out[rs, cs], inv_row[rs, :], inv_col[:, cs], len_row[rs, :],
                    len_col[:, cs], row_ids[rs, :], col_ids[:, cs],
                )

            return carry

        lax.fori_loop(0, tile_rows // CHUNK_ROWS * across, chunk, 0)


def split(value):
    high = value.astype(jnp.bfloat16)
    return high, (value - high.astype(jnp.float32)).astype(jnp.bfloat16)


def update_kernel(
    row_block, col_block, kernel, panel_row, panel_col, col_index, row_ids, col_ids, out
):
    tile_rows, tile_cols = out.shape
    top = pl.program_id(0) * tile_rows
    left = pl.program_id(1) * tile_cols
    needed = (top + tile_rows - 1) // row_block >= left // col_block

    @pl.when(needed)
    def _():
        row_high, row_low = split(panel_row[...])
        col_high, col_low = split(in_order(panel_col))
        mul = functools.partial(
            lax.dot_general, dimension_numbers=NT, preferred_element_type=jnp.float32
        )
        product = mul(row_high, col_high) + (mul(row_high, col_low) + mul(row_low, col_high))
        result = kernel[...] - product
        out[...] = jnp.where(row_ids[...] >= col_ids[...], result, 0.0)

    @pl.when(jnp.logical_not(needed))
    def _():
        out[...] = jnp.zeros_like(out)

    for member in range(PANEL // col_block):

        @pl.when(jnp.logical_and(left == 0, col_index[0] == member))
        def _():
            part = panel_row[:, member * col_block : (member + 1) * col_block]
            below = row_ids[...] >= col_ids[:, :col_block]
            out[:, :col_block] = jnp.where(below, part, 0.0)


def per_device(samples):
    row_count = lax.axis_size("row")
    col_count = lax.axis_size("col")
    share_count = row_count // col_count
    row_index = lax.axis_index("row")
    col_index = lax.axis_index("col")
    row_block = PANEL // row_count
    col_block = PANEL // col_count
    share_rows, feat_count = samples.shape
    rows_dev = share_rows * col_count
    cols_dev = rows_dev * share_count
    blocks = rows_dev // row_block
    moves = [
        (
            r * col_count + c,
            ((r % share_count) * col_count + c) * col_count + r // share_count,
        )
        for r in range(row_count)
        for c in range(col_count)
    ]

    def spread(moved):
        whole = lax.all_gather(moved, "row", axis=0, tiled=True)
        return whole.reshape(share_count, blocks, row_block, moved.shape[1])

    lead = samples[:row_block]
    held = jnp.where(col_index == 0, lead, jnp.zeros_like(lead))
    for target in range(1, col_count):
        held = held + lax.ppermute(lead, "col", [(0, target)])
    corner_feats = lax.all_gather(held, "row", axis=0, tiled=True)

    moved_feats = lax.ppermute(samples, ("row", "col"), moves)
    row_feats = lax.all_gather(samples, "col", axis=0, tiled=True)
    col_feats = spread(moved_feats)

    local_rows = jnp.arange(rows_dev, dtype=jnp.int32)
    row_ids = local_rows // row_block * PANEL + row_index * row_block + local_rows % row_block
    local_cols = jnp.arange(cols_dev, dtype=jnp.int32)
    col_ids = local_cols // col_block * PANEL + col_index * col_block + local_cols % col_block
    share_ids = lax.dynamic_slice_in_dim(row_ids, col_index * share_rows, share_rows, 0)
    lead_ids = jnp.arange(PANEL, dtype=jnp.int32)

    stacked = jnp.concatenate([corner_feats, samples], axis=0)
    stacked_ids = jnp.concatenate([lead_ids, share_ids], axis=0)
    inv, length = lengths(stacked)
    vmem = pl.BlockSpec(memory_space=pltpu.VMEM)
    solved = pl.pallas_call(
        panel_kernel,
        out_shape=jax.ShapeDtypeStruct((share_rows, PANEL), jnp.float32),
        in_specs=[vmem] * 7 + [pl.BlockSpec(memory_space=pl.ANY)],
        out_specs=vmem,
        scratch_shapes=[
            pltpu.VMEM((PANEL + share_rows, PANEL), jnp.float32),
            pltpu.VMEM((FACTOR, 2 * FACTOR), jnp.float32),
        ],
        compiler_params=pltpu.CompilerParams(vmem_limit_bytes=VMEM_LIMIT),
        cost_estimate=pl.CostEstimate(
            flops=80_000_000_000, bytes_accessed=4_000_000, transcendentals=0
        ),
    )(
        stacked, inv[:, None], inv[None, :PANEL], length[:, None], length[None, :PANEL],
        stacked_ids[:, None], lead_ids[None, :], moved_feats,
    )

    panel_row = lax.all_gather(solved, "col", axis=0, tiled=True)
    panel_col = spread(lax.ppermute(solved, ("row", "col"), moves))

    row_inv, row_len = lengths(row_feats)
    col_inv, col_len = lengths(col_feats.reshape(cols_dev, feat_count))
    col_inv, col_len = (
        value.reshape(share_count, blocks, row_block).transpose(1, 0, 2).reshape(cols_dev)
        for value in (col_inv, col_len)
    )
    tile_rows = min(TILE_ROWS, rows_dev)
    tile_cols = min(TILE_COLS, cols_dev)
    grid = (rows_dev // tile_rows, cols_dev // tile_cols)
    row_one = pl.BlockSpec((tile_rows, 1), lambda i, j: (i, 0))
    col_one = pl.BlockSpec((1, tile_cols), lambda i, j: (0, j))
    tile = pl.BlockSpec((tile_rows, tile_cols), lambda i, j: (i, j))

    def pieces(width):
        shape = (share_count, tile_cols // col_block, row_block, width)
        return pl.BlockSpec(shape, lambda i, j: (0, j, 0, 0))

    params = pltpu.CompilerParams(vmem_limit_bytes=VMEM_LIMIT)
    out_shape = jax.ShapeDtypeStruct((rows_dev, cols_dev), jnp.float32)
    kernel = pl.pallas_call(
        functools.partial(ntk_kernel, row_block, col_block),
        out_shape=out_shape,
        grid=grid,
        in_specs=[
            pl.BlockSpec((tile_rows, feat_count), lambda i, j: (i, 0)),
            pieces(feat_count),
            row_one, col_one, row_one, col_one, row_one, col_one,
            pl.BlockSpec(memory_space=pl.ANY),
        ],
        out_specs=tile,
        compiler_params=params,
        cost_estimate=pl.CostEstimate(
            flops=100_000_000_000, bytes_accessed=16_000_000, transcendentals=0
        ),
    )(
        row_feats, col_feats, row_inv[:, None], col_inv[None, :], row_len[:, None],
        col_len[None, :], row_ids[:, None], col_ids[None, :], solved,
    )
    return pl.pallas_call(
        functools.partial(update_kernel, row_block, col_block),
        out_shape=out_shape,
        grid=grid,
        in_specs=[
            tile,
            pl.BlockSpec((tile_rows, PANEL), lambda i, j: (i, 0)),
            pieces(PANEL),
            pl.BlockSpec(memory_space=pltpu.SMEM),
            row_one, col_one,
        ],
        out_specs=tile,
        input_output_aliases={0: 0},
        compiler_params=params,
        cost_estimate=pl.CostEstimate(
            flops=5_000_000_000, bytes_accessed=20_000_000, transcendentals=0
        ),
    )(kernel, panel_row, panel_col, col_index.astype(jnp.int32)[None], row_ids[:, None], col_ids[None, :])


def solution(mesh):
    return jax.shard_map(
        per_device,
        mesh=mesh,
        in_specs=(P(("row", "col"), None),),
        out_specs=P("row", "col"),
        check_vma=False,
    )
```

profile of v0, /device:TPU:1, one launch (start us, length us, event | category | flops | bytes accessed | tf_op | source)
XLA Modules:
  0.0 281.4 jit_solution(17772356049665732455)
XLA Ops:
  6.5 0.0 copy-start.4
  6.5 0.0 all-gather.5.cloned.1.call-start
  6.5 0.7 all-gather.5.cloned.1.call-update
  7.3 0.0 all-gather.7.cloned.1.call-start
  7.3 0.9 slice.9
  8.2 5.0 %collective-permute-start.2 = (bf16[64,768]{1,0:T(8,128)(2,1)S(1)}, bf16[64,768]{1,0:T(8,128)(2,1)S(1)}, u32[]{:S(2)}, u32[]{:S(2)}) collective-permute-start(bf16[64,768]{1,0:T(8,128)(2,1)S(1)} %slice.9), channel_id=1, source_target_pairs={{0,2},{4,6},{8,10},{12,14},{16,18},{20,22},{24,26},{28,30}} | collective-permute-start | bytes 294920 | tf_op jit(solution)/shard_map/ppermute | solution.py:261
  13.2 1.3 collective-permute-start.1
  14.6 1.3 collective-permute-start.3
  15.9 4.0 %collective-permute-start = (bf16[256,768]{1,0:T(8,128)(2,1)}, bf16[256,768]{1,0:T(8,128)(2,1)S(1)}, u32[]{:S(2)}, u32[]{:S(2)}) collective-permute-start(bf16[256,768]{1,0:T(8,128)(2,1)} %param.1), channel_id=1, source_target_pairs={{0,0},{1,4},{2,8},{3,12},{4,16},{5,20},{6,24},{7,28},{8,1},{9,5},{... | collective-permute-start | bytes 1179656 | tf_op jit(solution)/shard_map/ppermute | solution.py:264
  19.9 0.1 dynamic_slice.3
  20.0 0.2 broadcast_in_dim.29.row_ids
  20.1 0.0 collective-permute-done.2
  20.1 0.0 collective-permute-done.1
  20.2 0.0 collective-permute-done.3
  20.2 0.9 add_add_fusion
  21.1 13.3 %all_gather.17 = bf16[512,768]{1,0:T(8,128)(2,1)S(1)} all-gather(bf16[64,768]{1,0:T(8,128)(2,1)S(1)} %add_add_fusion), channel_id=1, replica_groups=mesh['row'=8,'col'=4] {'row'}, dimensions={0}, use_global_device_ids=true | all-gather | bytes 884736 | tf_op jit(solution)/shard_map/all_gather | solution.py:262
  34.4 0.1 constant_dynamic-update-slice_fusion.1
  34.5 0.0 copy-done.4
  34.5 0.3 multiply_reduce_fusion.2
  34.8 0.2 rsqrt.39.inv_row
  35.0 0.2 mul.111.len_row
  35.2 31.6 %collective-permute-done.after = bf16[256,768]{1,0:T(8,128)(2,1)S(1)} collective-permute-done((bf16[256,768]{1,0:T(8,128)(2,1)}, bf16[256,768]{1,0:T(8,128)(2,1)S(1)}, u32[]{:S(2)}, u32[]{:S(2)}) %collective-permute-start) | collective-permute-done | bytes 393248 | tf_op jit(solution)/shard_map/ppermute | solution.py:264
  66.8 0.0 copy-start.2
  66.8 0.7 copy-done.2
  67.6 0.0 all-gather.7.cloned.1.call-update
  67.6 0.0 all-gather.9.cloned.1.call-start
  67.6 0.0 copy-start.3
  67.7 1.0 copy-done.3
  68.6 65.7 %shard_map.17.after = f32[256,512]{1,0:T(8,128)} custom-call(bf16[768,768]{1,0:T(8,128)(2,1)S(1)} %constant_dynamic-update-slice_fusion.feats, f32[768,1]{1,0:T(8,128)S(1)} %rsqrt.39.inv_row, f32[1,512]{1,0:T(1,128)S(1)} %bitcast.9, f32[768,1]{1,0:T(8,128)S(1)} %mul.111.len_row, f32[1,512]{1,0:T(1,128)S(1)} %bitcast.10, ...), custom_call_target="tpu_custom_call" | custom-call | flops 80000000000 | bytes 4000000 | tf_op jit(solution)/shard_map/pallas_call | solution.py:279
  134.4 0.0 all-gather.9.cloned.1.call-update
  134.4 0.0 all-gather.11.cloned.1.call-start
  134.5 1.9 collective-permute-start.4
  136.4 0.1 fusion.8.row_ids
  136.5 52.2 %collective-permute-done.4 = f32[256,512]{1,0:T(8,128)S(1)} collective-permute-done((f32[256,512]{1,0:T(8,128)}, f32[256,512]{1,0:T(8,128)S(1)}, u32[]{:S(2)}, u32[]{:S(2)}) %collective-permute-start.4) | collective-permute-done | bytes 524320 | tf_op jit(solution)/shard_map/ppermute | solution.py:298
  188.7 0.0 copy-start.5
  188.7 0.8 copy-done.5
  189.5 0.0 all-gather.11.cloned.1.call-update
  189.6 0.0 all-gather.5.cloned.1.call-done.row_feats
  189.6 1.8 multiply_reduce_fusion.1
  191.4 0.0 copy-start.1
  191.4 0.2 copy.8.inv_row
  191.7 0.2 copy.9.len_row
  191.9 0.0 all-gather.7.cloned.1.call-done
  191.9 2.6 multiply_reduce_fusion
  194.5 0.1 mul.97
  194.6 0.1 broadcast_in_dim_reshape.7.len_col
  194.7 0.1 rsqrt.36
  194.8 0.1 broadcast_in_dim_reshape.6.inv_col
  194.9 0.0 copy-done.1
  194.9 59.0 %shard_map.18.kernel = f32[1024,2048]{1,0:T(8,128)} custom-call(bf16[1024,768]{1,0:T(8,128)(2,1)S(1)} %copy-done.1, bf16[2,16,64,768]{3,2,1,0:T(8,128)(2,1)} %bitcast.12, f32[1024,1]{1,0:T(8,128)S(1)} %copy.8.inv_row, f32[1,2048]{1,0:T(1,128)S(1)} %broadcast_in_dim_reshape.6.inv_col, f32[1024,1]{1,0:T(8,128)S(1)} %copy.9.len_row, ...), custom_call_target="tpu_custom_call" | custom-call | flops 99999997952 | bytes 16000000 | tf_op jit(solution)/shard_map/pallas_call | solution.py:319
  253.9 0.0 all-gather.9.cloned.1.call-done.panel_row
  253.9 0.0 all-gather.11.cloned.1.call-done
  253.9 0.0 copy-start
  253.9 1.6 copy-done
  255.5 19.4 %shard_map.19 = f32[1024,2048]{1,0:T(8,128)} custom-call(f32[1024,2048]{1,0:T(8,128)} %shard_map.18.kernel, f32[1024,512]{1,0:T(8,128)S(1)} %copy-done, f32[2,16,64,512]{3,2,1,0:T(8,128)} %bitcast.11, s32[1]{0:T(128)} %bitcast.8.col_index, s32[1024,1]{1,0:T(8,128)S(1)} %fusion.8.row_ids, s32[1,2048]{1,0:T(1,128)S(1)} %fusion.10.col_ids), custom_call_target="tpu_custom_call", output_to_operand_aliasing={{}: (0, {})} | custom-call | flops 5000000000 | bytes 20000000 | tf_op jit(solution)/shard_map/pallas_call | solution.py:338
  (13 shorter events, 0.1 us)
Async XLA Ops:
  6.5 27.9 %copy-start.4 = (bf16[256,768]{1,0:T(8,128)(2,1)S(1)}, bf16[256,768]{1,0:T(8,128)(2,1)}, u32[]{:S(2)}) copy-start(bf16[256,768]{1,0:T(8,128)(2,1)} %param.1) | copy-start | bytes 1179652
  6.5 183.0 %all-gather.5.cloned.1.call-start = ((), (), s32[]{:S(2)}) async-start(), calls=%async_computation | async-start | bytes 1966080 | tf_op jit(solution)/shard_map/all_gather | solution.py:265
  7.3 184.7 %all-gather.7.cloned.1.call-start = ((), (), s32[]{:S(2)}) async-start(), calls=%async_computation.1 | async-start | bytes 3538944 | tf_op jit(solution)/shard_map/all_gather | solution.py:255
  8.2 11.9 %collective-permute-start.2 = (bf16[64,768]{1,0:T(8,128)(2,1)S(1)}, bf16[64,768]{1,0:T(8,128)(2,1)S(1)}, u32[]{:S(2)}, u32[]{:S(2)}) collective-permute-start(bf16[64,768]{1,0:T(8,128)(2,1)S(1)} %slice.9), channel_id=1, source_target_pairs={{0,2},{4,6},{8,10},{12,14},{16,18},{20,22},{24,26},{28,30}} | collective-permute-start | bytes 294920 | tf_op jit(solution)/shard_map/ppermute | solution.py:261
  13.2 6.9 %collective-permute-start.1 = (bf16[64,768]{1,0:T(8,128)(2,1)S(1)}, bf16[64,768]{1,0:T(8,128)(2,1)S(1)}, u32[]{:S(2)}, u32[]{:S(2)}) collective-permute-start(bf16[64,768]{1,0:T(8,128)(2,1)S(1)} %slice.9), channel_id=1, source_target_pairs={{0,1},{4,5},{8,9},{12,13},{16,17},{20,21},{24,25},{28,29}} | collective-permute-start | bytes 294920 | tf_op jit(solution)/shard_map/ppermute | solution.py:261
  14.6 5.6 %collective-permute-start.3 = (bf16[64,768]{1,0:T(8,128)(2,1)S(1)}, bf16[64,768]{1,0:T(8,128)(2,1)S(1)}, u32[]{:S(2)}, u32[]{:S(2)}) collective-permute-start(bf16[64,768]{1,0:T(8,128)(2,1)S(1)} %slice.9), channel_id=1, source_target_pairs={{0,3},{4,7},{8,11},{12,15},{16,19},{20,23},{24,27},{28,31}} | collective-permute-start | bytes 294920 | tf_op jit(solution)/shard_map/ppermute | solution.py:261
  15.9 51.0 %collective-permute-start = (bf16[256,768]{1,0:T(8,128)(2,1)}, bf16[256,768]{1,0:T(8,128)(2,1)S(1)}, u32[]{:S(2)}, u32[]{:S(2)}) collective-permute-start(bf16[256,768]{1,0:T(8,128)(2,1)} %param.1), channel_id=1, source_target_pairs={{0,0},{1,4},{2,8},{3,12},{4,16},{5,20},{6,24},{7,28},{8,1},{9,5},{... | collective-permute-start | bytes 1179656 | tf_op jit(solution)/shard_map/ppermute | solution.py:264
  66.8 0.7 copy-start.2
  67.6 186.3 %all-gather.9.cloned.1.call-start = ((), (), s32[]{:S(2)}) async-start(), calls=%async_computation.2 | async-start | bytes 2621440 | tf_op jit(solution)/shard_map/all_gather | solution.py:297
  67.6 1.0 copy-start.3
  134.4 119.5 %all-gather.11.cloned.1.call-start = ((), (), s32[]{:S(2)}) async-start(), calls=%async_computation.3 | async-start | bytes 4718592 | tf_op jit(solution)/shard_map/all_gather | solution.py:255
  134.5 54.3 %collective-permute-start.4 = (f32[256,512]{1,0:T(8,128)}, f32[256,512]{1,0:T(8,128)S(1)}, u32[]{:S(2)}, u32[]{:S(2)}) collective-permute-start(f32[256,512]{1,0:T(8,128)} %shard_map.17.after), channel_id=1, source_target_pairs={{0,0},{1,4},{2,8},{3,12},{4,16},{5,20},{6,24},{7,28},{8,1},{9,5},{... | collective-permute-start | bytes 1572872 | tf_op jit(solution)/shard_map/ppermute | solution.py:298
  188.7 0.8 copy-start.5
  191.4 3.5 %copy-start.1 = (bf16[1024,768]{1,0:T(8,128)(2,1)S(1)}, bf16[1024,768]{1,0:T(8,128)(2,1)}, u32[]{:S(2)}) copy-start(bf16[1024,768]{1,0:T(8,128)(2,1)} %all-gather.5.cloned.1.call-done.row_feats) | copy-start | bytes 4718596
  253.9 1.6 copy-start
Sparse Core Ops, SparseCore 0:
  8.9 63.2 all-gather.4
  74.1 32.6 all-gather.6
  134.5 60.2 all-gather.8
  196.6 35.2 all-gather.10
where the time goes:
time: 282 us; the launch traced here: 281 us
  Pallas kernels  144 us (51%)
  waiting for transfers between devices  84.6 us (30%)
  starting transfers between devices  13.7 us (5%)
  between operations  13.4 us (5%)
  blocking collectives  13.3 us (5%)
  local copies, waits for them, and re-layouts  6.47 us (2%)
  other arithmetic  5.77 us (2%)
    pallas_call x1, Pallas kernels, per_device(): pl.pallas_call(panel_kernel, out_shape=jax.ShapeDtypeStruct((share_rows,...  65.7 us
    pallas_call x1, Pallas kernels, per_device(): pl.pallas_call(functools.partial(ntk_kernel, row_block, col_block), out_s...  59 us
    ppermute x1, waiting for transfers between devices, per_device(): panel_col = spread(lax.ppermute(solved, ('row', 'col'), moves))  52.2 us
    ppermute x1, waiting for transfers between devices, per_device(): moved_feats = lax.ppermute(samples, ('row', 'col'), moves)  31.6 us
    pallas_call x1, Pallas kernels, per_device(): pl.pallas_call(functools.partial(update_kernel, row_block, col_block), ou...  19.4 us
    all_gather x1, blocking collectives, per_device(): corner_feats = lax.all_gather(held, 'row', axis=0, tiled=True)  13.3 us
    ppermute x3, starting transfers between devices, per_device(): held = held + lax.ppermute(lead, 'col', [(0, target)])  7.63 us
  transfers between devices with their start and end apart: 9, of which 2 were waited for; matrix products, arithmetic and copies ran while one was open for 3% of the time, Pallas kernels for 44%

commit v1 on v0

v1 whole, which is shorter than its diff:
```python
import functools
import math

import jax
import jax.numpy as jnp
import numpy as np
from jax import lax
from jax.experimental import pallas as pl
from jax.experimental.pallas import tpu as pltpu
from jax.sharding import PartitionSpec as P

PANEL = 512
LAYERS = 8
CHUNK_ROWS = 64
CHUNK_COLS = 128
TILE_COLS = 512
FACTOR = 128
STRIP = 32
INV_PI = 1.0 / math.pi


def half_turns(reach):
    grid = np.linspace(1e-6, reach, 4001)
    want = 2.0 * np.arcsin(np.sqrt(grid / 2.0)) / (np.sqrt(grid) * math.pi)
    for degree in range(3, 10):
        fit = np.polynomial.Chebyshev.interpolate(
            lambda gap: 2.0 * np.arcsin(np.sqrt(gap / 2.0)) / (np.sqrt(gap) * math.pi),
            degree,
            domain=[0.0, reach],
        ).convert(kind=np.polynomial.Polynomial)
        if np.max(np.abs(fit(grid) - want)) < 4e-8:
            break
    return tuple(float(c) for c in fit.coef)


def layer_polynomials():
    least, found = 0.0, [half_turns(1.0)]
    for _ in range(LAYERS - 1):
        found.append(half_turns(min(1.0, 1.001 - least)))
        angle = math.acos(least)
        least = (math.sin(angle) + (math.pi - angle) * least) / math.pi
    return found


POLYNOMIALS = layer_polynomials()
VMEM_LIMIT = 24 * 1024 * 1024
HIGHEST = lax.Precision.HIGHEST
NT = (((1,), (1,)), ((), ()))
TN = (((0,), (0,)), ((), ()))


def angle_parts(size, polynomial):
    gap = jnp.maximum(1.0 - size, 1e-30)
    root = gap * lax.rsqrt(gap)
    poly = jnp.full_like(size, polynomial[-1])
    for coefficient in polynomial[-2::-1]:
        poly = poly * gap + coefficient
    wide = size * (INV_PI * INV_PI) + (INV_PI * INV_PI)
    sine = root * (wide * lax.rsqrt(wide))
    return root * poly, sine


def tangent_of(raw, on_diag):
    cosine = jnp.where(on_diag, 1.0, raw)
    tangent = raw
    turn, sine = angle_parts(jnp.abs(cosine), POLYNOMIALS[0])
    keep = jnp.where(cosine < 0.0, turn, 1.0 - turn)
    cosine = sine + keep * cosine
    tangent = cosine + tangent * keep
    for polynomial in POLYNOMIALS[1:]:
        turn, sine = angle_parts(cosine, polynomial)
        keep = 1.0 - turn
        cosine = sine + keep * cosine
        tangent = cosine + tangent * keep
    return tangent


def ntk_chunk(gram, inv_row, inv_col, len_row, len_col, row_ids, col_ids):
    on_diag = row_ids == col_ids
    raw = gram * inv_row * inv_col
    value = tangent_of(raw, on_diag) * (len_row * len_col)
    return value + jnp.where(on_diag, 1.0, 0.0)


def lengths(feats):
    wide = feats.astype(jnp.float32)
    total = jnp.sum(wide * wide, axis=1, keepdims=True)
    scale = math.sqrt(feats.shape[1] * (LAYERS + 1.0))
    return lax.rsqrt(total), jnp.sqrt(total) * (1.0 / scale)


def factor_strip(left, right, first):
    place = lax.broadcasted_iota(jnp.int32, (8, FACTOR), 0)
    groups = len(left)
    for g in range(groups):
        cols = [
            [
                jnp.broadcast_to(left[h][:, lane : lane + 1], (8, FACTOR))
                for h in range(g, groups)
            ]
            for lane in range(first + 8 * g, first + 8 * g + 8)
        ]
        for m in range(8):
            inv = lax.rsqrt(cols[m][0][m : m + 1, :])
            scaled = [col * inv for col in cols[m]]
            for n in range(m + 1, 8):
                factor = scaled[0][n : n + 1, :]
                cols[n] = [col - part * factor for col, part in zip(cols[n], scaled)]
            unit_left = left[g][m : m + 1, :] * inv
            unit_right = right[g][m : m + 1, :] * inv
            own = scaled[0]
            scaled[0] = jnp.where(place > m, own, jnp.where(place == m, own - 1.0, 0.0))
            for h in range(g, groups):
                left[h] = left[h] - scaled[h - g] * unit_left
                right[h] = right[h] - scaled[h - g] * unit_right
    return left, right


def panel_kernel(
    feats, inv_row, inv_col, len_row, len_col, row_ids, col_ids, after, work, inverses, both
):
    share_chunks = (feats.shape[0] - PANEL) // CHUNK_ROWS
    work[...] = lax.dot_general(
        feats[...], feats[:PANEL, :], NT, preferred_element_type=jnp.float32
    )
    across = PANEL // CHUNK_COLS

    def fill(rs, cs):
        work[rs, cs] = ntk_chunk(
            work[rs, cs], inv_row[rs, :], inv_col[:, cs], len_row[rs, :], len_col[:, cs],
            row_ids[rs, :], col_ids[:, cs],
        )

    def chunk(k, carry):
        r = k // across
        c = k % across

        @pl.when((r * CHUNK_ROWS) // FACTOR <= (c * CHUNK_COLS) // FACTOR)
        def _():
            fill(
                pl.ds(pl.multiple_of(r * CHUNK_ROWS, CHUNK_ROWS), CHUNK_ROWS),
                pl.ds(pl.multiple_of(c * CHUNK_COLS, CHUNK_COLS), CHUNK_COLS),
            )

        return carry

    lax.fori_loop(0, PANEL // CHUNK_ROWS * across, chunk, 0)
    eye = jnp.where(
        lax.broadcasted_iota(jnp.int32, (FACTOR, FACTOR), 0)
        == lax.broadcasted_iota(jnp.int32, (FACTOR, FACTOR), 1),
        1.0,
        0.0,
    )
    for start in range(0, PANEL, FACTOR):
        stop = start + FACTOR
        both[:, :FACTOR] = work[start:stop, start:stop]
        both[:, FACTOR:] = eye
        for first in range(0, FACTOR, STRIP):
            for q in range(first // STRIP, share_chunks, FACTOR // STRIP):
                own = PANEL + q * CHUNK_ROWS
                fill(pl.ds(own, CHUNK_ROWS), pl.ds(start, FACTOR))
            strip = both[first : first + STRIP, :]
            left, right = factor_strip(
                [strip[r : r + 8, :FACTOR] for r in range(0, STRIP, 8)],
                [strip[r : r + 8, FACTOR:] for r in range(0, STRIP, 8)],
                first,
            )
            left = jnp.concatenate(left, axis=0)
            strip = jnp.concatenate([left, jnp.concatenate(right, axis=0)], axis=1)
            both[first : first + STRIP, :] = strip
            last = first + STRIP
            if last < FACTOR:
                change = lax.dot_general(
                    left, strip, TN, precision=HIGHEST,
                    preferred_element_type=jnp.float32,
                )
                both[last:, :] = both[last:, :] - change[last:, :]
        inverse = both[:, FACTOR:]
        inverses[start:stop, :] = inverse
        if stop < PANEL:
            upper = jnp.dot(
                inverse, work[start:stop, stop:], precision=HIGHEST,
                preferred_element_type=jnp.float32,
            )
            work[stop:PANEL, stop:] = work[stop:PANEL, stop:] - lax.dot_general(
                upper, upper, TN, precision=HIGHEST, preferred_element_type=jnp.float32
            )
            work[start:stop, stop:] = upper


def solve_kernel(work, inverses, *rest):
    out = rest[-1]
    for start in range(0, PANEL, FACTOR):
        stop = start + FACTOR
        part = work[PANEL:, start:stop]
        if start:
            part = part - jnp.dot(
                out[:, :start], work[:start, start:stop], precision=HIGHEST,
                preferred_element_type=jnp.float32,
            )
        out[:, start:stop] = lax.dot_general(
            part, inverses[start:stop, :], NT, precision=HIGHEST,
            preferred_element_type=jnp.float32,
        )


def in_order(pieces):
    shares, blocks = pieces.shape[:2]
    return jnp.concatenate([pieces[s, b] for b in range(blocks) for s in range(shares)], axis=0)


def first_needed(j, tile_rows, tile_cols, row_block, col_block):
    return j * tile_cols // col_block * row_block // tile_rows


def ntk_kernel(
    row_block, col_block, col_feats, inv_col, len_col, row_ids, col_ids, col_index, after, *rest
):
    *pieces, out, row_feats, inv_row, len_row = rest
    tile_rows, tile_cols = out.shape
    i = pl.program_id(1)
    top = i * tile_rows
    left = pl.program_id(0) * tile_cols
    across = tile_cols // CHUNK_COLS
    count = len(pieces)

    for step, piece in enumerate(pieces):

        @pl.when(jnp.logical_and(left == 0, (col_index[0] - i + count) % count == step))
        def _():
            row_feats[i] = piece[...]
            inv, length = lengths(piece[...])
            inv_row[i] = inv
            len_row[i] = length

    @pl.when((top + tile_rows - 1) // row_block >= left // col_block)
    def _():
        out[...] = lax.dot_general(
            row_feats[i], in_order(col_feats), NT, preferred_element_type=jnp.float32
        )

        def chunk(k, carry):
            r = (k // across) * CHUNK_ROWS
            c = (k % across) * CHUNK_COLS
            below = (top + r + CHUNK_ROWS - 1) // row_block >= (left + c) // col_block
            beyond = left + c + CHUNK_COLS > col_block

            @pl.when(jnp.logical_and(below, beyond))
            def _():
                rs = pl.ds(pl.multiple_of(r, CHUNK_ROWS), CHUNK_ROWS)
                cs = pl.ds(pl.multiple_of(c, CHUNK_COLS), CHUNK_COLS)
                out[rs, cs] = ntk_chunk(
                    out[rs, cs], inv_row[i, rs, :], inv_col[:, cs], len_row[i, rs, :],
                    len_col[:, cs], row_ids[rs, :], col_ids[:, cs],
                )

            return carry

        lax.fori_loop(0, tile_rows // CHUNK_ROWS * across, chunk, 0)


def split(value):
    high = value.astype(jnp.bfloat16)
    return high, (value - high.astype(jnp.float32)).astype(jnp.bfloat16)


def update_kernel(
    row_block, col_block, kernel, panel_col, col_index, row_ids, col_ids, *rest
):
    *pieces, out, row_high, row_low = rest
    tile_rows, tile_cols = out.shape
    i = pl.program_id(1)
    top = i * tile_rows
    left = pl.program_id(0) * tile_cols
    needed = (top + tile_rows - 1) // row_block >= left // col_block
    count = len(pieces)

    for step, piece in enumerate(pieces):

        @pl.when(jnp.logical_and(left == 0, (col_index[0] - i + count) % count == step))
        def _():
            row_high[i], row_low[i] = split(piece[...])

    @pl.when(needed)
    def _():
        col_high, col_low = split(in_order(panel_col))
        mul = functools.partial(
            lax.dot_general, dimension_numbers=NT, preferred_element_type=jnp.float32
        )
        high, low = row_high[i], row_low[i]
        product = mul(high, col_high) + (mul(high, col_low) + mul(low, col_high))
        result = kernel[...] - product
        out[...] = jnp.where(row_ids[...] >= col_ids[...], result, 0.0)

    @pl.when(jnp.logical_not(needed))
    def _():
        out[...] = jnp.zeros_like(out)

    for member in range(count):
        for step, piece in enumerate(pieces):

            @pl.when(
                (left == 0) & (col_index[0] == member) & ((member - i + count) % count == step)
            )
            def _():
                part = piece[:, member * col_block : (member + 1) * col_block]
                below = row_ids[...] >= col_ids[:, :col_block]
                out[:, :col_block] = jnp.where(below, part, 0.0)


def per_device(samples):
    row_count = lax.axis_size("row")
    col_count = lax.axis_size("col")
    share_count = row_count // col_count
    row_index = lax.axis_index("row")
    col_index = lax.axis_index("col")
    row_block = PANEL // row_count
    col_block = PANEL // col_count
    share_rows, feat_count = samples.shape
    rows_dev = share_rows * col_count
    cols_dev = rows_dev * share_count
    blocks = rows_dev // row_block
    moves = [
        (
            r * col_count + c,
            ((r % share_count) * col_count + c) * col_count + r // share_count,
        )
        for r in range(row_count)
        for c in range(col_count)
    ]

    def spread(moved):
        whole = lax.all_gather(moved, "row", axis=0, tiled=True)
        return whole.reshape(share_count, blocks, row_block, moved.shape[1])

    lead = samples[:row_block]
    held = jnp.where(col_index == 0, lead, jnp.zeros_like(lead))
    for target in range(1, col_count):
        held = held + lax.ppermute(lead, "col", [(0, target)])
    corner_feats = lax.all_gather(held, "row", axis=0, tiled=True)

    def pass_along(share):
        return [share] + [
            lax.ppermute(share, "col", [(k, (k + s) % col_count) for k in range(col_count)])
            for s in range(1, col_count)
        ]

    late_samples, _ = lax.optimization_barrier((samples, held))
    moved_feats = lax.ppermute(late_samples, ("row", "col"), moves)
    row_feats = pass_along(late_samples)
    col_feats = spread(moved_feats)

    local_rows = jnp.arange(rows_dev, dtype=jnp.int32)
    row_ids = local_rows // row_block * PANEL + row_index * row_block + local_rows % row_block
    local_cols = jnp.arange(cols_dev, dtype=jnp.int32)
    col_ids = local_cols // col_block * PANEL + col_index * col_block + local_cols % col_block
    share_ids = lax.dynamic_slice_in_dim(row_ids, col_index * share_rows, share_rows, 0)
    lead_ids = jnp.arange(PANEL, dtype=jnp.int32)

    stacked = jnp.concatenate([corner_feats, samples], axis=0)
    stacked_ids = jnp.concatenate([lead_ids, share_ids], axis=0)
    inv, length = lengths(stacked)
    vmem = pl.BlockSpec(memory_space=pltpu.VMEM)
    work, inverses = pl.pallas_call(
        panel_kernel,
        out_shape=[
            jax.ShapeDtypeStruct((PANEL + share_rows, PANEL), jnp.float32),
            jax.ShapeDtypeStruct((PANEL, FACTOR), jnp.float32),
        ],
        in_specs=[vmem] * 7 + [pl.BlockSpec(memory_space=pl.ANY)],
        out_specs=[vmem, vmem],
        scratch_shapes=[
            pltpu.VMEM((FACTOR, 2 * FACTOR), jnp.float32),
        ],
        compiler_params=pltpu.CompilerParams(vmem_limit_bytes=VMEM_LIMIT),
        cost_estimate=pl.CostEstimate(
            flops=80_000_000_000, bytes_accessed=4_000_000, transcendentals=0
        ),
    )(
        stacked, inv, inv[:PANEL].reshape(1, PANEL), length, length[:PANEL].reshape(1, PANEL),
        stacked_ids[:, None], lead_ids[None, :], moved_feats,
    )
    solved = pl.pallas_call(
        solve_kernel,
        out_shape=jax.ShapeDtypeStruct((share_rows, PANEL), jnp.float32),
        in_specs=[vmem] * 2 + [pl.BlockSpec(memory_space=pl.ANY)] * (col_count - 1),
        out_specs=vmem,
        compiler_params=pltpu.CompilerParams(vmem_limit_bytes=VMEM_LIMIT),
        cost_estimate=pl.CostEstimate(
            flops=5_000_000_000, bytes_accessed=4_000_000, transcendentals=0
        ),
    )(work, inverses, *row_feats[1:])

    panel_row = pass_along(solved)
    panel_col = spread(lax.ppermute(solved, ("row", "col"), moves))

    col_inv, col_len = lengths(col_feats.reshape(cols_dev, feat_count))
    col_inv, col_len = (
        value.reshape(share_count, blocks, row_block).transpose(1, 0, 2).reshape(1, cols_dev)
        for value in (col_inv, col_len)
    )
    tile_rows = share_rows
    tile_cols = min(TILE_COLS, cols_dev)
    grid = (cols_dev // tile_cols, rows_dev // tile_rows)
    first = functools.partial(
        first_needed, tile_rows=tile_rows, tile_cols=tile_cols, row_block=row_block,
        col_block=col_block,
    )
    row_one = pl.BlockSpec((tile_rows, 1), lambda j, i: (i, 0))
    col_one = pl.BlockSpec((1, tile_cols), lambda j, i: (0, j))
    tile = pl.BlockSpec((tile_rows, tile_cols), lambda j, i: (i, j))
    needed_tile = pl.BlockSpec(
        (tile_rows, tile_cols), lambda j, i: (jnp.maximum(i, first(j)), j)
    )
    scalar = pl.BlockSpec(memory_space=pltpu.SMEM)
    col_place = col_index.astype(jnp.int32)[None]

    def share(width):
        return pl.BlockSpec((share_rows, width), lambda j, i: (0, 0))

    def pieces(width):
        shape = (share_count, tile_cols // col_block, row_block, width)
        return pl.BlockSpec(shape, lambda j, i: (0, j, 0, 0))

    params = pltpu.CompilerParams(vmem_limit_bytes=VMEM_LIMIT)
    out_shape = jax.ShapeDtypeStruct((rows_dev, cols_dev), jnp.float32)
    kernel = pl.pallas_call(
        functools.partial(ntk_kernel, row_block, col_block),
        out_shape=out_shape,
        grid=grid,
        in_specs=[
            pieces(feat_count),
            col_one, col_one, row_one, col_one, scalar,
            pl.BlockSpec(memory_space=pl.ANY),
        ]
        + [share(feat_count)] * col_count,
        out_specs=needed_tile,
        scratch_shapes=[
            pltpu.VMEM((col_count, share_rows, feat_count), jnp.bfloat16),
            pltpu.VMEM((col_count, share_rows, 1), jnp.float32),
            pltpu.VMEM((col_count, share_rows, 1), jnp.float32),
        ],
        compiler_params=params,
        cost_estimate=pl.CostEstimate(
            flops=100_000_000_000, bytes_accessed=16_000_000, transcendentals=0
        ),
    )(
        col_feats, col_inv, col_len, row_ids[:, None], col_ids[None, :], col_place, solved,
        *row_feats,
    )

    return pl.pallas_call(
        functools.partial(update_kernel, row_block, col_block),
        out_shape=out_shape,
        grid=grid,
        in_specs=[
            needed_tile,
            pieces(PANEL),
            scalar,
            row_one, col_one,
        ]
        + [share(PANEL)] * col_count,
        out_specs=tile,
        scratch_shapes=[
            pltpu.VMEM((col_count, share_rows, PANEL), jnp.bfloat16),
            pltpu.VMEM((col_count, share_rows, PANEL), jnp.bfloat16),
        ],
        compiler_params=params,
        cost_estimate=pl.CostEstimate(
            flops=5_000_000_000, bytes_accessed=20_000_000, transcendentals=0
        ),
    )(kernel, panel_col, col_place, row_ids[:, None], col_ids[None, :], *panel_row)


def solution(mesh):
    return jax.shard_map(
        per_device,
        mesh=mesh,
        in_specs=(P(("row", "col"), None),),
        out_specs=P("row", "col"),
        check_vma=False,
    )
```

time: 282 us -> 249 us (0.88)
  the two profiles are of different devices: /device:TPU:1 before, /device:TPU:14 now
where the time goes in v1:
time: 249 us; the launch traced here: 248 us
  Pallas kernels  97.9 us (39%)
  waiting for transfers between devices  78.3 us (31%)
  local copies, waits for them, and re-layouts  22.8 us (9%)
  starting transfers between devices  19.6 us (8%)
  between operations  13.7 us (6%)
  blocking collectives  9.95 us (4%)
  other arithmetic  5.48 us (2%)
    pallas_call x1, Pallas kernels, per_device(): pl.pallas_call(functools.partial(ntk_kernel, row_block, col_block), out_s...  49.6 us
    ppermute x1, waiting for transfers between devices, per_device(): panel_col = spread(lax.ppermute(solved, ('row', 'col'), moves))  35.8 us
    ppermute x1, waiting for transfers between devices, per_device(): moved_feats = lax.ppermute(late_samples, ('row', 'col'), moves)  34.8 us
    pallas_call x1, Pallas kernels, per_device(): pl.pallas_call(panel_kernel, out_shape=[jax.ShapeDtypeStruct((PANEL + sha...  28.9 us
    pallas_call x1, Pallas kernels, per_device(): pl.pallas_call(functools.partial(update_kernel, row_block, col_block), ou...  16.2 us
    unnamed x23, local copies, waits for them, and re-layouts  14.3 us
    all_gather x1, blocking collectives, per_device(): corner_feats = lax.all_gather(held, 'row', axis=0, tiled=True)  9.95 us
    ppermute x6, starting transfers between devices, pass_along(): lax.ppermute(share, 'col', [(k, (k + s) % col_count) for k in range(col_c...  8.62 us
  transfers between devices with their start and end apart: 13, of which 3 were waited for; matrix products, arithmetic and copies ran while one was open for 5% of the time, Pallas kernels for 33%

profile of v1, /device:TPU:14, one launch (start us, length us, event | category | flops | bytes accessed | tf_op | source)
XLA Modules:
  0.0 247.7 jit_solution(18434734699549754172)
XLA Ops:
  6.5 0.0 all-gather.3.cloned.1.call-start
  6.5 1.0 slice.11
  7.5 0.7 collective-permute-start.1
  8.2 1.3 collective-permute-start
  9.5 0.7 collective-permute-start.2
  10.2 0.1 dynamic_slice.3
  10.3 0.2 broadcast_in_dim.9.row_ids
  10.4 0.0 collective-permute-done.1
  10.4 7.6 %collective-permute-done = bf16[64,768]{1,0:T(8,128)(2,1)S(1)} collective-permute-done((bf16[64,768]{1,0:T(8,128)(2,1)S(1)}, bf16[64,768]{1,0:T(8,128)(2,1)S(1)}, u32[]{:S(2)}, u32[]{:S(2)}) %collective-permute-start) | collective-permute-done | bytes 98336 | tf_op jit(solution)/shard_map/ppermute | solution.py:339
  18.0 0.0 collective-permute-done.2
  18.0 0.9 add_add_fusion
  18.9 0.8 collective-permute-start.6
  19.7 2.9 %collective-permute-start.5 = (bf16[256,768]{1,0:T(8,128)(2,1)}, bf16[256,768]{1,0:T(8,128)(2,1)}, u32[]{:S(2)}, u32[]{:S(2)}) collective-permute-start(bf16[256,768]{1,0:T(8,128)(2,1)} %rest_0_), channel_id=1, source_target_pairs={{0,2},{1,3},{2,0},{3,1},{4,6},{5,7},{6,4},{7,5},{8,10},{9,11},{10,... | collective-permute-start | bytes 1179656 | tf_op jit(solution)/shard_map/ppermute | solution.py:344
  22.6 2.8 %collective-permute-start.4 = (bf16[256,768]{1,0:T(8,128)(2,1)}, bf16[256,768]{1,0:T(8,128)(2,1)}, u32[]{:S(2)}, u32[]{:S(2)}) collective-permute-start(bf16[256,768]{1,0:T(8,128)(2,1)} %rest_0_), channel_id=1, source_target_pairs={{0,1},{1,2},{2,3},{3,0},{4,5},{5,6},{6,7},{7,4},{8,9},{9,10},{10,1... | collective-permute-start | bytes 1179656 | tf_op jit(solution)/shard_map/ppermute | solution.py:344
  25.5 1.9 collective-permute-start.3
  27.4 9.9 %all_gather.10 = bf16[512,768]{1,0:T(8,128)(2,1)S(1)} all-gather(bf16[64,768]{1,0:T(8,128)(2,1)S(1)} %add_add_fusion), channel_id=1, replica_groups=mesh['row'=8,'col'=4] {'row'}, dimensions={0}, use_global_device_ids=true | all-gather | bytes 884736 | tf_op jit(solution)/shard_map/all_gather | solution.py:340
  37.4 0.1 constant_dynamic-update-slice_fusion.1
  37.4 0.0 copy-done.6
  37.5 0.3 multiply_reduce_fusion.1
  37.8 0.2 rsqrt.18.inv_row
  38.0 0.2 mul.82.len_row
  38.1 34.8 %collective-permute-done.3.after = bf16[256,768]{1,0:T(8,128)(2,1)S(1)} collective-permute-done((bf16[256,768]{1,0:T(8,128)(2,1)}, bf16[256,768]{1,0:T(8,128)(2,1)S(1)}, u32[]{:S(2)}, u32[]{:S(2)}) %collective-permute-start.3) | collective-permute-done | bytes 393248 | tf_op jit(solution)/shard_map/ppermute | solution.py:349
  73.0 0.7 copy-done.7
  73.7 0.0 all-gather.3.cloned.1.call-update
  73.7 0.0 all-gather.5.cloned.1.call-start
  73.8 0.0 copy-start.8
  73.8 1.0 copy-done.8
  74.8 28.9 %shard_map.17 = (f32[768,512]{1,0:T(8,128)S(1)}, f32[512,128]{1,0:T(8,128)S(1)}) custom-call(bf16[768,768]{1,0:T(8,128)(2,1)S(1)} %constant_dynamic-update-slice_fusion.feats, f32[768,1]{1,0:T(8,128)S(1)} %rsqrt.18.inv_row, f32[1,512]{1,0:T(1,128)S(1)} %bitcast.9, f32[768,1]{1,0:T(8,128)S(1)} %mul.82.len_row, f32[1,512]{1,0:T(1,128)S(1)} %bitcast.10, ...), custom_call_target="tpu_custom_call" | custom-call | flops 80000000000 | bytes 4000000 | tf_op jit(solution)/shard_map/pallas_call | solution.py:364
  103.7 0.0 collective-permute-done.6.rest_2_.rest_3_
  103.7 0.0 collective-permute-done.5.rest_1_.rest_2_
  103.7 0.0 collective-permute-done.4.rest_0_.rest_1_
  103.7 3.2 %shard_map.18.after.rest_0_ = f32[256,512]{1,0:T(8,128)} custom-call(f32[768,512]{1,0:T(8,128)S(1)} %get-tuple-element.9.work, f32[512,128]{1,0:T(8,128)S(1)} %get-tuple-element.10.inverses, bf16[256,768]{1,0:T(8,128)(2,1)} %collective-permute-done.4.rest_0_.rest_1_, bf16[256,768]{1,0:T(8,128)(2,1)} %collective-permute-done.5.rest_1_.rest_2_, ...), custom_call_target="tpu_custom_call" | custom-call | flops 5000000000 | bytes 4000000 | tf_op jit(solution)/shard_map/pallas_call | solution.py:383
  106.9 6.4 %collective-permute-start.7 = (f32[256,512]{1,0:T(8,128)}, f32[256,512]{1,0:T(8,128)S(1)}, u32[]{:S(2)}, u32[]{:S(2)}) collective-permute-start(f32[256,512]{1,0:T(8,128)} %shard_map.18.after.rest_0_), channel_id=1, source_target_pairs={{0,0},{1,4},{2,8},{3,12},{4,16},{5,20},{6,24},{7,28},{8,1},{9,5},{... | collective-permute-start | bytes 1572872 | tf_op jit(solution)/shard_map/ppermute | solution.py:395
  113.3 0.9 fusion.8.row_ids
  114.3 0.1 collective-permute-start.10
  114.3 0.1 collective-permute-start.9
  114.4 1.9 collective-permute-start.8
  116.3 35.8 %collective-permute-done.7 = f32[256,512]{1,0:T(8,128)S(1)} collective-permute-done((f32[256,512]{1,0:T(8,128)}, f32[256,512]{1,0:T(8,128)S(1)}, u32[]{:S(2)}, u32[]{:S(2)}) %collective-permute-start.7) | collective-permute-done | bytes 524320 | tf_op jit(solution)/shard_map/ppermute | solution.py:395
  152.2 0.8 copy-done.10
  153.0 0.0 all-gather.5.cloned.1.call-update
  153.0 0.0 all-gather.3.cloned.1.call-done
  153.0 0.0 copy-start.3
  153.0 2.7 %multiply_reduce_fusion = f32[2048]{0:T(1024)S(1)} fusion(bf16[2048,768]{1,0:T(8,128)(2,1)} %all-gather.3.cloned.1.call-done), kind=kLoop, calls=%fused_computation | loop fusion | flops 4716544 | bytes 3153920 | tf_op jit(solution)/shard_map/reduce_sum | solution.py:87
  155.8 0.6 sqrt_multiply_fusion
  156.4 0.7 mul.68
  157.1 1.3 copy.3
  158.4 0.8 reshape.177.len_col
  159.2 1.4 rsqrt.15
  160.6 1.3 copy.2
  161.9 1.4 reshape.176.inv_col
  163.3 0.0 copy-done.3
  163.3 1.0 copy-done.4
  164.4 0.7 copy-done.9
  165.1 49.6 %shard_map.19.kernel = f32[1024,2048]{1,0:T(8,128)S(1)} custom-call(bf16[2,16,64,768]{3,2,1,0:T(8,128)(2,1)S(1)} %bitcast.8, f32[1,2048]{1,0:T(1,128)S(1)} %copy-done.9, f32[1,2048]{1,0:T(1,128)S(1)} %reshape.177.len_col, s32[1024,1]{1,0:T(8,128)S(1)} %copy-done.4, s32[1,2048]{1,0:T(1,128)S(1)} %fusion.10.col_ids, s32[1]{0:T(128)} %bitcast.3.col_index, ...), custom_call_target="tpu_custom_call" | custom-call | flops 99999997952 | bytes 16000000 | tf_op jit(solution)/shard_map/pallas_call | solution.py:427
  214.6 0.0 copy-start
  214.7 3.4 %copy-done = f32[1024,2048]{1,0:T(8,128)} copy-done((f32[1024,2048]{1,0:T(8,128)}, f32[1024,2048]{1,0:T(8,128)S(1)}, u32[]{:S(2)}) %copy-start) | copy-done | bytes 8388632
  218.0 0.0 collective-permute-done.10.rest_3_
  218.0 0.0 collective-permute-done.9.rest_2_
  218.0 0.0 collective-permute-done.8.rest_1_
  218.1 0.0 all-gather.5.cloned.1.call-done
  218.1 3.4 %copy-done.1 = f32[1024,2048]{1,0:T(8,128)S(1)} copy-done((f32[1024,2048]{1,0:T(8,128)S(1)}, f32[1024,2048]{1,0:T(8,128)}, u32[]{:S(2)}) %copy-start.1) | copy-done | bytes 8388632
  221.5 2.2 copy-done.2
  223.7 1.0 copy-done.5
  224.7 16.2 %shard_map.20 = f32[1024,2048]{1,0:T(8,128)} custom-call(f32[1024,2048]{1,0:T(8,128)S(1)} %copy-done.1, f32[2,16,64,512]{3,2,1,0:T(8,128)S(1)} %bitcast.7, s32[1]{0:T(128)} %bitcast.3.col_index, s32[1024,1]{1,0:T(8,128)S(1)} %copy-done.5, s32[1,2048]{1,0:T(1,128)S(1)} %fusion.10.col_ids, f32[256,512]{1,0:T(8,128)} %shard_map.18.after.rest_0_, ...), custom_call_target="tpu_custom_call" | custom-call | flops 5000000000 | bytes 20000000 | tf_op jit(solution)/shard_map/pallas_call | solution.py:452
  (17 shorter events, 0.1 us)
Async XLA Ops:
  6.5 30.9 %copy-start.6 = (bf16[256,768]{1,0:T(8,128)(2,1)S(1)}, bf16[256,768]{1,0:T(8,128)(2,1)}, u32[]{:S(2)}) copy-start(bf16[256,768]{1,0:T(8,128)(2,1)} %rest_0_) | copy-start | bytes 1179652
  6.5 146.5 %all-gather.3.cloned.1.call-start = ((), (), s32[]{:S(2)}) async-start(), calls=%async_computation | async-start | bytes 3538944 | tf_op jit(solution)/shard_map/all_gather | solution.py:333
  7.5 2.9 %collective-permute-start.1 = (bf16[64,768]{1,0:T(8,128)(2,1)S(1)}, bf16[64,768]{1,0:T(8,128)(2,1)S(1)}, u32[]{:S(2)}, u32[]{:S(2)}) collective-permute-start(bf16[64,768]{1,0:T(8,128)(2,1)S(1)} %slice.11), channel_id=1, source_target_pairs={{0,2},{4,6},{8,10},{12,14},{16,18},{20,22},{24,26},{28,30}} | collective-permute-start | bytes 294920 | tf_op jit(solution)/shard_map/ppermute | solution.py:339
  8.2 9.8 %collective-permute-start = (bf16[64,768]{1,0:T(8,128)(2,1)S(1)}, bf16[64,768]{1,0:T(8,128)(2,1)S(1)}, u32[]{:S(2)}, u32[]{:S(2)}) collective-permute-start(bf16[64,768]{1,0:T(8,128)(2,1)S(1)} %slice.11), channel_id=1, source_target_pairs={{0,1},{4,5},{8,9},{12,13},{16,17},{20,21},{24,25},{28,29}} | collective-permute-start | bytes 294920 | tf_op jit(solution)/shard_map/ppermute | solution.py:339
  9.5 8.5 %collective-permute-start.2 = (bf16[64,768]{1,0:T(8,128)(2,1)S(1)}, bf16[64,768]{1,0:T(8,128)(2,1)S(1)}, u32[]{:S(2)}, u32[]{:S(2)}) collective-permute-start(bf16[64,768]{1,0:T(8,128)(2,1)S(1)} %slice.11), channel_id=1, source_target_pairs={{0,3},{4,7},{8,11},{12,15},{16,19},{20,23},{24,27},{28,31}} | collective-permute-start | bytes 294920 | tf_op jit(solution)/shard_map/ppermute | solution.py:339
  18.9 84.8 %collective-permute-start.6 = (bf16[256,768]{1,0:T(8,128)(2,1)}, bf16[256,768]{1,0:T(8,128)(2,1)}, u32[]{:S(2)}, u32[]{:S(2)}) collective-permute-start(bf16[256,768]{1,0:T(8,128)(2,1)} %rest_0_), channel_id=1, source_target_pairs={{0,3},{1,0},{2,1},{3,2},{4,7},{5,4},{6,5},{7,6},{8,11},{9,8},{10,9... | collective-permute-start | bytes 1179656 | tf_op jit(solution)/shard_map/ppermute | solution.py:344
  19.7 84.0 %collective-permute-start.5 = (bf16[256,768]{1,0:T(8,128)(2,1)}, bf16[256,768]{1,0:T(8,128)(2,1)}, u32[]{:S(2)}, u32[]{:S(2)}) collective-permute-start(bf16[256,768]{1,0:T(8,128)(2,1)} %rest_0_), channel_id=1, source_target_pairs={{0,2},{1,3},{2,0},{3,1},{4,6},{5,7},{6,4},{7,5},{8,10},{9,11},{10,... | collective-permute-start | bytes 1179656 | tf_op jit(solution)/shard_map/ppermute | solution.py:344
  22.6 81.1 %collective-permute-start.4 = (bf16[256,768]{1,0:T(8,128)(2,1)}, bf16[256,768]{1,0:T(8,128)(2,1)}, u32[]{:S(2)}, u32[]{:S(2)}) collective-permute-start(bf16[256,768]{1,0:T(8,128)(2,1)} %rest_0_), channel_id=1, source_target_pairs={{0,1},{1,2},{2,3},{3,0},{4,5},{5,6},{6,7},{7,4},{8,9},{9,10},{10,1... | collective-permute-start | bytes 1179656 | tf_op jit(solution)/shard_map/ppermute | solution.py:344
  25.5 47.5 %collective-permute-start.3 = (bf16[256,768]{1,0:T(8,128)(2,1)}, bf16[256,768]{1,0:T(8,128)(2,1)S(1)}, u32[]{:S(2)}, u32[]{:S(2)}) collective-permute-start(bf16[256,768]{1,0:T(8,128)(2,1)} %rest_0_), channel_id=1, source_target_pairs={{0,0},{1,4},{2,8},{3,12},{4,16},{5,20},{6,24},{7,28},{8,1},{9,5},{... | collective-permute-start | bytes 1179656 | tf_op jit(solution)/shard_map/ppermute | solution.py:349
  72.9 0.7 copy-start.7
  73.7 144.4 %all-gather.5.cloned.1.call-start = ((), (), s32[]{:S(2)}) async-start(), calls=%async_computation.1 | async-start | bytes 4718592 | tf_op jit(solution)/shard_map/all_gather | solution.py:333
  73.8 1.0 copy-start.8
  106.9 45.2 %collective-permute-start.7 = (f32[256,512]{1,0:T(8,128)}, f32[256,512]{1,0:T(8,128)S(1)}, u32[]{:S(2)}, u32[]{:S(2)}) collective-permute-start(f32[256,512]{1,0:T(8,128)} %shard_map.18.after.rest_0_), channel_id=1, source_target_pairs={{0,0},{1,4},{2,8},{3,12},{4,16},{5,20},{6,24},{7,28},{8,1},{9,5},{... | collective-permute-start | bytes 1572872 | tf_op jit(solution)/shard_map/ppermute | solution.py:395
  114.3 103.8 %collective-permute-start.10 = (f32[256,512]{1,0:T(8,128)}, f32[256,512]{1,0:T(8,128)}, u32[]{:S(2)}, u32[]{:S(2)}) collective-permute-start(f32[256,512]{1,0:T(8,128)} %shard_map.18.after.rest_0_), channel_id=1, source_target_pairs={{0,3},{1,0},{2,1},{3,2},{4,7},{5,4},{6,5},{7,6},{8,11},{9,8},{10,9... | collective-permute-start | bytes 1572872 | tf_op jit(solution)/shard_map/ppermute | solution.py:344
  114.3 103.7 %collective-permute-start.9 = (f32[256,512]{1,0:T(8,128)}, f32[256,512]{1,0:T(8,128)}, u32[]{:S(2)}, u32[]{:S(2)}) collective-permute-start(f32[256,512]{1,0:T(8,128)} %shard_map.18.after.rest_0_), channel_id=1, source_target_pairs={{0,2},{1,3},{2,0},{3,1},{4,6},{5,7},{6,4},{7,5},{8,10},{9,11},{10,... | collective-permute-start | bytes 1572872 | tf_op jit(solution)/shard_map/ppermute | solution.py:344
  114.4 103.7 %collective-permute-start.8 = (f32[256,512]{1,0:T(8,128)}, f32[256,512]{1,0:T(8,128)}, u32[]{:S(2)}, u32[]{:S(2)}) collective-permute-start(f32[256,512]{1,0:T(8,128)} %shard_map.18.after.rest_0_), channel_id=1, source_target_pairs={{0,1},{1,2},{2,3},{3,0},{4,5},{5,6},{6,7},{7,4},{8,9},{9,10},{10,1... | collective-permute-start | bytes 1572872 | tf_op jit(solution)/shard_map/ppermute | solution.py:344
  152.2 0.8 copy-start.10
  153.0 10.3 %copy-start.3 = (bf16[2048,768]{1,0:T(8,128)(2,1)S(1)}, bf16[2048,768]{1,0:T(8,128)(2,1)}, u32[]{:S(2)}) copy-start(bf16[2048,768]{1,0:T(8,128)(2,1)} %all-gather.3.cloned.1.call-done) | copy-start | bytes 9437188
  163.3 1.0 copy-start.4
  164.4 0.7 copy-start.9
  214.6 3.4 %copy-start = (f32[1024,2048]{1,0:T(8,128)}, f32[1024,2048]{1,0:T(8,128)S(1)}, u32[]{:S(2)}) copy-start(f32[1024,2048]{1,0:T(8,128)S(1)} %shard_map.19.kernel) | copy-start | bytes 25165828
  218.1 3.4 %copy-start.1 = (f32[1024,2048]{1,0:T(8,128)S(1)}, f32[1024,2048]{1,0:T(8,128)}, u32[]{:S(2)}) copy-start(f32[1024,2048]{1,0:T(8,128)} %copy-done) | copy-start | bytes 25165828
  221.5 2.2 copy-start.2
  223.7 1.0 copy-start.5
Sparse Core Ops, SparseCore 0:
  73.8 32.6 all-gather.2
  153.1 34.9 all-gather.4

commit v2 on v1

--- a/solution.py
+++ b/solution.py
@@ -214,9 +214,9 @@
 
 
 def ntk_kernel(
-    row_block, col_block, col_feats, inv_col, len_col, row_ids, col_ids, col_index, after, *rest
+    row_block, col_block, col_feats, row_ids, col_ids, col_index, after, *rest
 ):
-    *pieces, out, row_feats, inv_row, len_row = rest
+    *pieces, out, row_feats, inv_row, len_row, inv_col, len_col = rest
     tile_rows, tile_cols = out.shape
     i = pl.program_id(1)
     top = i * tile_rows
@@ -233,6 +233,16 @@
             inv_row[i] = inv
             len_row[i] = length
 
+    @pl.when(i == 0)
+    def _():
+        wide = in_order(col_feats).astype(jnp.float32)
+        high, low = split(wide * wide)
+        ones = jnp.ones((8, wide.shape[1]), jnp.bfloat16)
+        total = lax.dot_general(ones, high, NT, preferred_element_type=jnp.float32)
+        total += lax.dot_general(ones, low, NT, preferred_element_type=jnp.float32)
+        inv_col[...] = lax.rsqrt(total)
+        len_col[...] = jnp.sqrt(total) * (1.0 / math.sqrt(wide.shape[1] * (LAYERS + 1.0)))
+
     @pl.when((top + tile_rows - 1) // row_block >= left // col_block)
     def _():
         out[...] = lax.dot_general(
@@ -250,8 +260,8 @@
                 rs = pl.ds(pl.multiple_of(r, CHUNK_ROWS), CHUNK_ROWS)
                 cs = pl.ds(pl.multiple_of(c, CHUNK_COLS), CHUNK_COLS)
                 out[rs, cs] = ntk_chunk(
-                    out[rs, cs], inv_row[i, rs, :], inv_col[:, cs], len_row[i, rs, :],
-                    len_col[:, cs], row_ids[rs, :], col_ids[:, cs],
+                    out[rs, cs], inv_row[i, rs, :], inv_col[:1, cs], len_row[i, rs, :],
+                    len_col[:1, cs], row_ids[rs, :], col_ids[:, cs],
                 )
 
             return carry
@@ -347,7 +357,8 @@
 
     late_samples, _ = lax.optimization_barrier((samples, held))
     moved_feats = lax.ppermute(late_samples, ("row", "col"), moves)
-    row_feats = pass_along(late_samples)
+    later_samples, moved_feats = lax.optimization_barrier((late_samples, moved_feats))
+    row_feats = pass_along(later_samples)
     col_feats = spread(moved_feats)
 
     local_rows = jnp.arange(rows_dev, dtype=jnp.int32)
@@ -391,14 +402,11 @@
         ),
     )(work, inverses, *row_feats[1:])
 
-    panel_row = pass_along(solved)
-    panel_col = spread(lax.ppermute(solved, ("row", "col"), moves))
-
-    col_inv, col_len = lengths(col_feats.reshape(cols_dev, feat_count))
-    col_inv, col_len = (
-        value.reshape(share_count, blocks, row_block).transpose(1, 0, 2).reshape(1, cols_dev)
-        for value in (col_inv, col_len)
-    )
+    moved_panel = lax.ppermute(solved, ("row", "col"), moves)
+    later_solved, moved_panel = lax.optimization_barrier((solved, moved_panel))
+    panel_row = pass_along(later_solved)
+    panel_col = spread(moved_panel)
+
     tile_rows = share_rows
     tile_cols = min(TILE_COLS, cols_dev)
     grid = (cols_dev // tile_cols, rows_dev // tile_rows)
@@ -422,7 +430,7 @@
         shape = (share_count, tile_cols // col_block, row_block, width)
         return pl.BlockSpec(shape, lambda j, i: (0, j, 0, 0))
 
-    params = pltpu.CompilerParams(vmem_limit_bytes=VMEM_LIMIT)
+    params = pltpu.CompilerParams(vmem_limit_bytes=2 * VMEM_LIMIT)
     out_shape = jax.ShapeDtypeStruct((rows_dev, cols_dev), jnp.float32)
     kernel = pl.pallas_call(
         functools.partial(ntk_kernel, row_block, col_block),
@@ -430,7 +438,7 @@
         grid=grid,
         in_specs=[
             pieces(feat_count),
-            col_one, col_one, row_one, col_one, scalar,
+            row_one, col_one, scalar,
             pl.BlockSpec(memory_space=pl.ANY),
         ]
         + [share(feat_count)] * col_count,
@@ -439,13 +447,15 @@
             pltpu.VMEM((col_count, share_rows, feat_count), jnp.bfloat16),
             pltpu.VMEM((col_count, share_rows, 1), jnp.float32),
             pltpu.VMEM((col_count, share_rows, 1), jnp.float32),
+            pltpu.VMEM((8, tile_cols), jnp.float32),
+            pltpu.VMEM((8, tile_cols), jnp.float32),
         ],
         compiler_params=params,
         cost_estimate=pl.CostEstimate(
             flops=100_000_000_000, bytes_accessed=16_000_000, transcendentals=0
         ),
     )(
-        col_feats, col_inv, col_len, row_ids[:, None], col_ids[None, :], col_place, solved,
+        col_feats, row_ids[:, None], col_ids[None, :], col_place, solved,
         *row_feats,
     )
 

time: 249 us -> 224 us (0.90)
  waiting for transfers between devices: 78.3 us -> 53.1 us
  starting transfers between devices: 19.6 us -> 39.6 us
  local copies, waits for them, and re-layouts: 22.8 us -> 5.28 us
  other arithmetic: 5.48 us -> 1.37 us
    ppermute x6, starting transfers between devices: 8.62 us -> 28.7 us  [pass_along(): lax.ppermute(share, 'col', [(k, (k + s) % col_count) for k in range(col_c...]
    ppermute x1, waiting for transfers between devices: 34.8 us -> 20.9 us  [per_device(): moved_feats = lax.ppermute(late_samples, ('row', 'col'), moves)]
    ppermute x1, waiting for transfers between devices: 35.8 us -> 24.5 us  [per_device(): moved_panel = lax.ppermute(solved, ('row', 'col'), moves)]
    unnamed x23 -> x11, local copies, waits for them, and re-layouts: 14.3 us -> 3.72 us
    ppermute x1, starting transfers between devices: 6.38 us -> 1.92 us  [per_device(): moved_panel = lax.ppermute(solved, ('row', 'col'), moves)]
    ppermute x1, starting transfers between devices: 1.91 us -> 6.33 us  [per_device(): moved_feats = lax.ppermute(late_samples, ('row', 'col'), moves)]
    pallas_call x1, Pallas kernels: 49.6 us -> 52.4 us  [per_device(): pl.pallas_call(functools.partial(ntk_kernel, row_block, col_block), out_s...]
    reduce_sum x2 -> x1, other arithmetic: 3.02 us -> 0.3 us  [lengths(): total = jnp.sum(wide * wide, axis=1, keepdims=True)]
  transfers between devices with their start and end apart: 13 -> 13, of which waited for: 3 -> 3; matrix products, arithmetic and copies ran while one was open for 5% -> 0% of each run, Pallas kernels for 33% -> 38%
where the time goes in v2:
time: 224 us; the launch traced here: 223 us
  Pallas kernels  100 us (45%)
  waiting for transfers between devices  53.1 us (24%)
  starting transfers between devices  39.6 us (18%)
  between operations  13.6 us (6%)
  blocking collectives  9.43 us (4%)
  local copies, waits for them, and re-layouts  5.28 us (2%)
    pallas_call x1, Pallas kernels, per_device(): pl.pallas_call(functools.partial(ntk_kernel, row_block, col_block), out_s...  52.4 us
    pallas_call x1, Pallas kernels, per_device(): pl.pallas_call(panel_kernel, out_shape=[jax.ShapeDtypeStruct((PANEL + sha...  28.9 us
    ppermute x6, starting transfers between devices, pass_along(): lax.ppermute(share, 'col', [(k, (k + s) % col_count) for k in range(col_c...  28.7 us
    ppermute x1, waiting for transfers between devices, per_device(): moved_panel = lax.ppermute(solved, ('row', 'col'), moves)  24.5 us
    ppermute x1, waiting for transfers between devices, per_device(): moved_feats = lax.ppermute(late_samples, ('row', 'col'), moves)  20.9 us
    pallas_call x1, Pallas kernels, per_device(): pl.pallas_call(functools.partial(update_kernel, row_block, col_block), ou...  16.5 us
    all_gather x1, blocking collectives, per_device(): corner_feats = lax.all_gather(held, 'row', axis=0, tiled=True)  9.43 us
    ppermute x3, waiting for transfers between devices, per_device(): held = held + lax.ppermute(lead, 'col', [(0, target)])  7.58 us
  transfers between devices with their start and end apart: 13, of which 3 were waited for; matrix products, arithmetic and copies ran while one was open for 0% of the time, Pallas kernels for 38%

profile of v2, /device:TPU:14, one launch (start us, length us, event | category | flops | bytes accessed | tf_op | source)
XLA Modules:
  0.0 222.6 jit_solution(9315160618064330101)
XLA Ops:
  6.5 0.0 copy-start
  6.5 0.0 all-gather.3.cloned.1.call-start
  6.5 1.0 slice.11
  7.5 0.7 collective-permute-start.1
  8.2 1.3 collective-permute-start
  9.5 0.7 collective-permute-start.2
  10.2 0.1 dynamic_slice.3
  10.3 0.2 broadcast_in_dim.18.row_ids
  10.4 0.0 collective-permute-done.1
  10.4 7.6 %collective-permute-done = bf16[64,768]{1,0:T(8,128)(2,1)S(1)} collective-permute-done((bf16[64,768]{1,0:T(8,128)(2,1)S(1)}, bf16[64,768]{1,0:T(8,128)(2,1)S(1)}, u32[]{:S(2)}, u32[]{:S(2)}) %collective-permute-start) | collective-permute-done | bytes 98336 | tf_op jit(solution)/shard_map/ppermute | solution.py:349
  18.0 0.0 collective-permute-done.2
  18.0 0.9 add_add_fusion
  18.9 9.4 %all_gather.10 = bf16[512,768]{1,0:T(8,128)(2,1)S(1)} all-gather(bf16[64,768]{1,0:T(8,128)(2,1)S(1)} %add_add_fusion), channel_id=1, replica_groups=mesh['row'=8,'col'=4] {'row'}, dimensions={0}, use_global_device_ids=true | all-gather | bytes 884736 | tf_op jit(solution)/shard_map/all_gather | solution.py:350
  28.4 0.0 copy-done
  28.4 6.3 %collective-permute-start.3 = (bf16[256,768]{1,0:T(8,128)(2,1)S(1)}, bf16[256,768]{1,0:T(8,128)(2,1)S(1)}, u32[]{:S(2)}, u32[]{:S(2)}) collective-permute-start(bf16[256,768]{1,0:T(8,128)(2,1)S(1)} %copy-done), channel_id=1, source_target_pairs={{0,0},{1,4},{2,8},{3,12},{4,16},{5,20},{6,24},{7,28},{8,1},{9,5},{... | collective-permute-start | bytes 1179656 | tf_op jit(solution)/shard_map/ppermute | solution.py:359
  34.7 0.1 constant_dynamic-update-slice_fusion.1
  34.8 0.3 multiply_reduce_fusion
  35.1 0.2 rsqrt.7.inv_row
  35.3 0.2 mul.63.len_row
  35.5 20.9 %collective-permute-done.3.after = bf16[256,768]{1,0:T(8,128)(2,1)S(1)} collective-permute-done((bf16[256,768]{1,0:T(8,128)(2,1)S(1)}, bf16[256,768]{1,0:T(8,128)(2,1)S(1)}, u32[]{:S(2)}, u32[]{:S(2)}) %collective-permute-start.3) | collective-permute-done | bytes 393248 | tf_op jit(solution)/shard_map/ppermute | solution.py:359
  56.3 0.0 copy-start.1
  56.3 0.0 collective-permute-start.6
  56.3 9.5 %collective-permute-start.5 = (bf16[256,768]{1,0:T(8,128)(2,1)S(1)}, bf16[256,768]{1,0:T(8,128)(2,1)}, u32[]{:S(2)}, u32[]{:S(2)}) collective-permute-start(bf16[256,768]{1,0:T(8,128)(2,1)S(1)} %copy-done), channel_id=1, source_target_pairs={{0,2},{1,3},{2,0},{3,1},{4,6},{5,7},{6,4},{7,5},{8,10},{9,11},{10,... | collective-permute-start | bytes 1179656 | tf_op jit(solution)/shard_map/ppermute | solution.py:354
  65.9 1.8 collective-permute-start.4
  67.7 0.0 copy-done.1
  67.7 0.0 all-gather.3.cloned.1.call-update
  67.7 0.0 all-gather.5.cloned.1.call-start
  67.8 0.0 copy-start.2
  67.8 1.0 copy-done.2
  68.8 28.9 %shard_map.17 = (f32[768,512]{1,0:T(8,128)S(1)}, f32[512,128]{1,0:T(8,128)S(1)}) custom-call(bf16[768,768]{1,0:T(8,128)(2,1)S(1)} %constant_dynamic-update-slice_fusion.feats, f32[768,1]{1,0:T(8,128)S(1)} %rsqrt.7.inv_row, f32[1,512]{1,0:T(1,128)S(1)} %bitcast.5, f32[768,1]{1,0:T(8,128)S(1)} %mul.63.len_row, f32[1,512]{1,0:T(1,128)S(1)} %bitcast.6, ...), custom_call_target="tpu_custom_call" | custom-call | flops 80000000000 | bytes 4000000 | tf_op jit(solution)/shard_map/pallas_call | solution.py:375
  97.7 0.0 collective-permute-done.6.rest_2_.rest_3_
  97.7 0.0 collective-permute-done.5.rest_1_.rest_2_
  97.7 0.0 collective-permute-done.4.rest_0_.rest_1_
  97.7 2.4 %shard_map.18.after.rest_0_ = f32[256,512]{1,0:T(8,128)S(1)} custom-call(f32[768,512]{1,0:T(8,128)S(1)} %get-tuple-element.14.work, f32[512,128]{1,0:T(8,128)S(1)} %get-tuple-element.15.inverses, bf16[256,768]{1,0:T(8,128)(2,1)} %collective-permute-done.4.rest_0_.rest_1_, bf16[256,768]{1,0:T(8,128)(2,1)} %collective-permute-done.5.rest_1_.rest_2_, ...), custom_call_target="tpu_custom_call" | custom-call | flops 5000000000 | bytes 4000000 | tf_op jit(solution)/shard_map/pallas_call | solution.py:394
  100.1 1.9 collective-permute-start.7
  102.1 0.1 fusion.8.row_ids
  102.2 24.5 %collective-permute-done.7 = f32[256,512]{1,0:T(8,128)S(1)} collective-permute-done((f32[256,512]{1,0:T(8,128)S(1)}, f32[256,512]{1,0:T(8,128)S(1)}, u32[]{:S(2)}, u32[]{:S(2)}) %collective-permute-start.7) | collective-permute-done | bytes 524320 | tf_op jit(solution)/shard_map/ppermute | solution.py:405
  126.7 0.0 copy-start.4
  126.7 0.8 copy-done.4
  127.5 0.0 collective-permute-start.10
  127.5 14.5 %collective-permute-start.9 = (f32[256,512]{1,0:T(8,128)S(1)}, f32[256,512]{1,0:T(8,128)S(1)}, u32[]{:S(2)}, u32[]{:S(2)}) collective-permute-start(f32[256,512]{1,0:T(8,128)S(1)} %shard_map.18.after.rest_0_), channel_id=1, source_target_pairs={{0,2},{1,3},{2,0},{3,1},{4,6},{5,7},{6,4},{7,5},{8,10},{9,11},{10,... | collective-permute-start | bytes 1572872 | tf_op jit(solution)/shard_map/ppermute | solution.py:354
  142.0 2.9 %collective-permute-start.8 = (f32[256,512]{1,0:T(8,128)S(1)}, f32[256,512]{1,0:T(8,128)S(1)}, u32[]{:S(2)}, u32[]{:S(2)}) collective-permute-start(f32[256,512]{1,0:T(8,128)S(1)} %shard_map.18.after.rest_0_), channel_id=1, source_target_pairs={{0,1},{1,2},{2,3},{3,0},{4,5},{5,6},{6,7},{7,4},{8,9},{9,10},{10,1... | collective-permute-start | bytes 1572872 | tf_op jit(solution)/shard_map/ppermute | solution.py:354
  144.9 0.0 all-gather.5.cloned.1.call-update
  145.0 0.0 all-gather.3.cloned.1.call-done
  145.0 0.0 copy-start.3
  145.0 1.9 copy-done.3
  146.9 52.4 %shard_map.19.kernel = f32[1024,2048]{1,0:T(8,128)} custom-call(bf16[2,16,64,768]{3,2,1,0:T(8,128)(2,1)S(1)} %bitcast.7, s32[1024,1]{1,0:T(8,128)S(1)} %fusion.8.row_ids, s32[1,2048]{1,0:T(1,128)S(1)} %fusion.10.col_ids, s32[1]{0:T(128)} %bitcast.1.col_index, f32[256,512]{1,0:T(8,128)S(1)} %shard_map.18.after.rest_0_, bf16[256,768]{1,0:T(8,128)(2,1)S(1)} %copy-done, ...), custom_call_target="tpu_custom_call" | custom-call | flops 99999997952 | bytes 16000000 | tf_op jit(solution)/shard_map/pallas_call | solution.py:435
  199.2 0.0 collective-permute-done.10.rest_3_
  199.2 0.0 collective-permute-done.9.rest_2_
  199.2 0.0 collective-permute-done.8.rest_1_
  199.2 0.0 all-gather.5.cloned.1.call-done
  199.3 16.5 %shard_map.20 = f32[1024,2048]{1,0:T(8,128)} custom-call(f32[1024,2048]{1,0:T(8,128)} %shard_map.19.kernel, f32[2,16,64,512]{3,2,1,0:T(8,128)} %bitcast.8, s32[1]{0:T(128)} %bitcast.1.col_index, s32[1024,1]{1,0:T(8,128)S(1)} %fusion.8.row_ids, s32[1,2048]{1,0:T(1,128)S(1)} %fusion.10.col_ids, f32[256,512]{1,0:T(8,128)S(1)} %shard_map.18.after.rest_0_, ...), custom_call_target="tpu_custom_call" | custom-call | flops 5000000000 | bytes 20000000 | tf_op jit(solution)/shard_map/pallas_call | solution.py:462
  (9 shorter events, 0.1 us)
Async XLA Ops:
  6.5 21.8 %copy-start = (bf16[256,768]{1,0:T(8,128)(2,1)S(1)}, bf16[256,768]{1,0:T(8,128)(2,1)}, u32[]{:S(2)}) copy-start(bf16[256,768]{1,0:T(8,128)(2,1)} %rest_0_) | copy-start | bytes 1179652
  6.5 138.4 %all-gather.3.cloned.1.call-start = ((), (), s32[]{:S(2)}) async-start(), calls=%async_computation | async-start | bytes 3538944 | tf_op jit(solution)/shard_map/all_gather | solution.py:343
  7.5 2.9 %collective-permute-start.1 = (bf16[64,768]{1,0:T(8,128)(2,1)S(1)}, bf16[64,768]{1,0:T(8,128)(2,1)S(1)}, u32[]{:S(2)}, u32[]{:S(2)}) collective-permute-start(bf16[64,768]{1,0:T(8,128)(2,1)S(1)} %slice.11), channel_id=1, source_target_pairs={{0,2},{4,6},{8,10},{12,14},{16,18},{20,22},{24,26},{28,30}} | collective-permute-start | bytes 294920 | tf_op jit(solution)/shard_map/ppermute | solution.py:349
  8.2 9.8 %collective-permute-start = (bf16[64,768]{1,0:T(8,128)(2,1)S(1)}, bf16[64,768]{1,0:T(8,128)(2,1)S(1)}, u32[]{:S(2)}, u32[]{:S(2)}) collective-permute-start(bf16[64,768]{1,0:T(8,128)(2,1)S(1)} %slice.11), channel_id=1, source_target_pairs={{0,1},{4,5},{8,9},{12,13},{16,17},{20,21},{24,25},{28,29}} | collective-permute-start | bytes 294920 | tf_op jit(solution)/shard_map/ppermute | solution.py:349
  9.5 8.5 %collective-permute-start.2 = (bf16[64,768]{1,0:T(8,128)(2,1)S(1)}, bf16[64,768]{1,0:T(8,128)(2,1)S(1)}, u32[]{:S(2)}, u32[]{:S(2)}) collective-permute-start(bf16[64,768]{1,0:T(8,128)(2,1)S(1)} %slice.11), channel_id=1, source_target_pairs={{0,3},{4,7},{8,11},{12,15},{16,19},{20,23},{24,27},{28,31}} | collective-permute-start | bytes 294920 | tf_op jit(solution)/shard_map/ppermute | solution.py:349
  28.4 28.0 %collective-permute-start.3 = (bf16[256,768]{1,0:T(8,128)(2,1)S(1)}, bf16[256,768]{1,0:T(8,128)(2,1)S(1)}, u32[]{:S(2)}, u32[]{:S(2)}) collective-permute-start(bf16[256,768]{1,0:T(8,128)(2,1)S(1)} %copy-done), channel_id=1, source_target_pairs={{0,0},{1,4},{2,8},{3,12},{4,16},{5,20},{6,24},{7,28},{8,1},{9,5},{... | collective-permute-start | bytes 1179656 | tf_op jit(solution)/shard_map/ppermute | solution.py:359
  56.3 11.3 %copy-start.1 = (bf16[256,768]{1,0:T(8,128)(2,1)}, bf16[256,768]{1,0:T(8,128)(2,1)S(1)}, u32[]{:S(2)}) copy-start(bf16[256,768]{1,0:T(8,128)(2,1)S(1)} %collective-permute-done.3.after) | copy-start | bytes 1179652
  56.3 41.3 %collective-permute-start.6 = (bf16[256,768]{1,0:T(8,128)(2,1)S(1)}, bf16[256,768]{1,0:T(8,128)(2,1)}, u32[]{:S(2)}, u32[]{:S(2)}) collective-permute-start(bf16[256,768]{1,0:T(8,128)(2,1)S(1)} %copy-done), channel_id=1, source_target_pairs={{0,3},{1,0},{2,1},{3,2},{4,7},{5,4},{6,5},{7,6},{8,11},{9,8},{10,9... | collective-permute-start | bytes 1179656 | tf_op jit(solution)/shard_map/ppermute | solution.py:354
  56.3 41.3 %collective-permute-start.5 = (bf16[256,768]{1,0:T(8,128)(2,1)S(1)}, bf16[256,768]{1,0:T(8,128)(2,1)}, u32[]{:S(2)}, u32[]{:S(2)}) collective-permute-start(bf16[256,768]{1,0:T(8,128)(2,1)S(1)} %copy-done), channel_id=1, source_target_pairs={{0,2},{1,3},{2,0},{3,1},{4,6},{5,7},{6,4},{7,5},{8,10},{9,11},{10,... | collective-permute-start | bytes 1179656 | tf_op jit(solution)/shard_map/ppermute | solution.py:354
  65.9 31.8 %collective-permute-start.4 = (bf16[256,768]{1,0:T(8,128)(2,1)S(1)}, bf16[256,768]{1,0:T(8,128)(2,1)}, u32[]{:S(2)}, u32[]{:S(2)}) collective-permute-start(bf16[256,768]{1,0:T(8,128)(2,1)S(1)} %copy-done), channel_id=1, source_target_pairs={{0,1},{1,2},{2,3},{3,0},{4,5},{5,6},{6,7},{7,4},{8,9},{9,10},{10,1... | collective-permute-start | bytes 1179656 | tf_op jit(solution)/shard_map/ppermute | solution.py:354
  67.7 131.6 %all-gather.5.cloned.1.call-start = ((), (), s32[]{:S(2)}) async-start(), calls=%async_computation.1 | async-start | bytes 4718592 | tf_op jit(solution)/shard_map/all_gather | solution.py:343
  67.8 1.0 copy-start.2
  100.1 26.6 %collective-permute-start.7 = (f32[256,512]{1,0:T(8,128)S(1)}, f32[256,512]{1,0:T(8,128)S(1)}, u32[]{:S(2)}, u32[]{:S(2)}) collective-permute-start(f32[256,512]{1,0:T(8,128)S(1)} %shard_map.18.after.rest_0_), channel_id=1, source_target_pairs={{0,0},{1,4},{2,8},{3,12},{4,16},{5,20},{6,24},{7,28},{8,1},{9,5},{... | collective-permute-start | bytes 1572872 | tf_op jit(solution)/shard_map/ppermute | solution.py:405
  126.7 0.8 copy-start.4
  127.5 71.7 %collective-permute-start.10 = (f32[256,512]{1,0:T(8,128)S(1)}, f32[256,512]{1,0:T(8,128)S(1)}, u32[]{:S(2)}, u32[]{:S(2)}) collective-permute-start(f32[256,512]{1,0:T(8,128)S(1)} %shard_map.18.after.rest_0_), channel_id=1, source_target_pairs={{0,3},{1,0},{2,1},{3,2},{4,7},{5,4},{6,5},{7,6},{8,11},{9,8},{10,9... | collective-permute-start | bytes 1572872 | tf_op jit(solution)/shard_map/ppermute | solution.py:354
  127.5 71.7 %collective-permute-start.9 = (f32[256,512]{1,0:T(8,128)S(1)}, f32[256,512]{1,0:T(8,128)S(1)}, u32[]{:S(2)}, u32[]{:S(2)}) collective-permute-start(f32[256,512]{1,0:T(8,128)S(1)} %shard_map.18.after.rest_0_), channel_id=1, source_target_pairs={{0,2},{1,3},{2,0},{3,1},{4,6},{5,7},{6,4},{7,5},{8,10},{9,11},{10,... | collective-permute-start | bytes 1572872 | tf_op jit(solution)/shard_map/ppermute | solution.py:354
  142.0 57.2 %collective-permute-start.8 = (f32[256,512]{1,0:T(8,128)S(1)}, f32[256,512]{1,0:T(8,128)S(1)}, u32[]{:S(2)}, u32[]{:S(2)}) collective-permute-start(f32[256,512]{1,0:T(8,128)S(1)} %shard_map.18.after.rest_0_), channel_id=1, source_target_pairs={{0,1},{1,2},{2,3},{3,0},{4,5},{5,6},{6,7},{7,4},{8,9},{9,10},{10,1... | collective-permute-start | bytes 1572872 | tf_op jit(solution)/shard_map/ppermute | solution.py:354
  145.0 1.9 copy-start.3
Sparse Core Ops, SparseCore 0:
  67.8 32.4 all-gather.2
  145.1 35.5 all-gather.4
